TPU v7x, 512 devices: a whole 4x4x16 slice. The times are simulated.
512 devices in a mesh: dp: 64 (over z, x_hi, core), rep: 8 (over y, x_lo).
Axes of the slice: x: 4 (x_hi: 2, x_lo: 2; x = x_hi * 2 + x_lo), y: 4, z: 16, core: 2. Of those that a mesh axis runs over, the one named last changes fastest.
Arguments:
- grad_out: bfloat16 [49152, 2048], P('dp', 'rep'), may hold values from -16 to 16
- pre_act: bfloat16 [49152, 3072], P('dp', 'rep'), may hold values from -6 to 6
- up_weight: bfloat16 [3072, 2048], P('rep'), may hold values from -0.125 to 0.125
- down_weight: bfloat16 [2048, 3072], P(None, 'rep'), may hold values from -0.109375 to 0.109375
- slot_counts: int32 [64], P('dp'), may hold values from 384 to 768, as said below
Outputs:
- input_grad: bfloat16 [49152, 2048], P('dp')
- down_grad: float32 [2048, 3072], P('dp', 'rep')
Inputs may be any that keep to these rules, and one draw needn't show every extreme that they name: Row i * 768 + j is live exactly when j < slot_counts[i]; some index has all 768 slots live and some index exactly 384.
All inputs are finite; a program needn't handle non-finite values.
Results may differ from a plain program's by a relative error of at most 0.0049.
Values may be sent and summed in bfloat16 or wider, within the bound.
No kernel may reach another device: no remote copies, remote signals or barrier semaphores. Data moves between devices by JAX's collectives and lax.ppermute only.
A program may use at most 64 MiB of HBM per device.

v0:
```python
import jax
import jax.numpy as jnp
from jax import lax
from jax.sharding import Mesh
from jax.sharding import PartitionSpec as P

REP = ("rep_0", "rep_1")


def whole_of(array, axes, dim):
    if not axes:
        return array
    nearer = lax.all_gather(array, axes[-1], axis=dim, tiled=True)
    return whole_of(nearer, axes[:-1], dim)


def on_device(grad_out, pre_act, up_weight, down_weight, slot_counts):
    slot_rows = grad_out.shape[0]
    live_rows = (lax.iota(jnp.int32, slot_rows) < slot_counts[0])[:, None]
    grad_full = whole_of(grad_out, REP, 1)
    grad_live = jnp.where(live_rows, grad_full, jnp.zeros_like(grad_full))
    zero_pre = jnp.zeros_like(pre_act)
    hidden = jnp.where(live_rows, jnp.maximum(pre_act, zero_pre), zero_pre)
    data_ranks = lax.axis_size("dp")
    down_sum = lax.psum_scatter(
        lax.dot_general(
            grad_live, hidden, (((0,), (0,)), ((), ())), preferred_element_type=jnp.float32
        ),
        "dp",
        scatter_dimension=0,
        tiled=True,
    )
    down_grad = down_sum / data_ranks
    hidden_grad = jnp.dot(grad_live, down_weight, preferred_element_type=jnp.float32)
    pre_grad = jnp.where(pre_act > 0, hidden_grad, jnp.zeros_like(hidden_grad)).astype(jnp.bfloat16)
    partial_terms = jnp.dot(pre_grad, up_weight, preferred_element_type=jnp.float32)
    input_sum = lax.psum(partial_terms, REP)
    input_grad = input_sum.astype(jnp.bfloat16)
    return (input_grad, down_grad)


def solution(mesh):
    finer = Mesh(mesh.devices.reshape(mesh.shape["dp"], 4, 2), ("dp", "rep_0", "rep_1"))
    in_specs = (P("dp", REP), P("dp", REP), P(REP, None), P(None, REP), P("dp"))
    out_specs = (P("dp", None), P("dp", REP))
    return jax.shard_map(
        on_device, mesh=finer, in_specs=in_specs, out_specs=out_specs, check_vma=False
    )
```

profile of v0, /device:TPU:4, one launch (start us, length us, event | category | flops | bytes accessed | tf_op | source)
XLA Modules:
  0.0 350.7 jit_solution(8490427789314710554)
XLA Ops:
  7.2 0.0 copy-start
  7.2 0.0 all-gather.2.cloned.1.call-start
  7.2 13.1 %all_gather.6 = bf16[768,512]{1,0:T(8,128)(2,1)} all-gather(bf16[768,256]{1,0:T(8,128)(2,1)} %param.5), channel_id=1, replica_groups=mesh['dp'=64,'rep_0'=4,'rep_1'=2] {'rep_1'}, dimensions={1}, use_global_device_ids=true | all-gather | bytes 1179648 | tf_op jit(solution)/shard_map/all_gather | solution.py:13
  20.3 0.0 all-gather.2.cloned.1.call-update
  20.4 0.0 reduce-scatter.2.cloned.1.call-start
  21.1 51.1 %all-gather.2.cloned.1.call-done = bf16[768,2048]{1,0:T(8,128)(2,1)} async-done(((bf16[768,512]{1,0:T(8,128)(2,1)}), bf16[768,2048]{1,0:T(8,128)(2,1)}) %all-gather.2.cloned.1.call-update) | async-done | bytes 3145744 | tf_op jit(solution)/shard_map/all_gather | solution.py:13
  72.2 5.6 %fusion.1 = f32[2048,384]{1,0:T(8,128)} fusion(bf16[768,2048]{1,0:T(8,128)(2,1)} %all-gather.2.cloned.1.call-done, pred[768]{0:T(1024)(128)(4,1)S(1)} %iota_compare_fusion, bf16[768,384]{1,0:T(8,128)(2,1)} %param.6), kind=kOutput, calls=%fused_computation.3 | convolution fusion | flops 1210122240 | bytes 6882048 | tf_op jit(solution)/shard_map/dot_general | solution.py:26
  77.8 0.0 copy-start.1
  77.8 0.0 reduce-scatter.2.cloned.1.call-update
  77.9 0.0 copy-done
  77.9 1.4 copy-done.1
  79.2 8.1 %fusion.2 = f32[768,2048]{1,0:T(8,128)} fusion(bf16[384,2048]{1,0:T(8,128)(2,1)S(1)} %copy-done, bf16[2048,384]{1,0:T(8,128)(2,1)S(1)} %copy-done.1, bf16[768,2048]{1,0:T(8,128)(2,1)} %all-gather.2.cloned.1.call-done, pred[768]{0:T(1024)(128)(4,1)S(1)} %iota_compare_fusion, bf16[768,384]{1,0:T(8,128)(2,1)} %param.6), kind=kOutput, calls=%fused_computation.4 | convolution fusion | flops 2418376704 | bytes 13173504 | tf_op jit(solution)/shard_map/dot_general | solution.py:36
  87.4 255.0 %all-reduce.1 = bf16[768,2048]{1,0:T(8,128)(2,1)} all-reduce(f32[768,2048]{1,0:T(8,128)} %fusion.2), channel_id=1, replica_groups=mesh['dp'=64,'rep_0'=4,'rep_1'=2] {'rep_0','rep_1'}, use_global_device_ids=true, to_apply=%region_0.1 | all-reduce | flops 1572864 | bytes 9437184 | tf_op jit(solution)/shard_map/psum | solution.py:37
  342.4 0.0 reduce-scatter.2.cloned.1.call-done
  342.4 1.4 broadcast_multiply_fusion
  (1 shorter events, 0.0 us)
Async XLA Ops:
  7.2 70.7 %copy-start = (bf16[384,2048]{1,0:T(8,128)(2,1)S(1)}, bf16[384,2048]{1,0:T(8,128)(2,1)}, u32[]{:S(2)}) copy-start(bf16[384,2048]{1,0:T(8,128)(2,1)} %param.7) | copy-start | bytes 4718596
  7.2 65.0 %all-gather.2.cloned.1.call-start = ((), (), s32[]{:S(2)}) async-start(), calls=%async_computation.1 | async-start | bytes 3932160 | tf_op jit(solution)/shard_map/all_gather | solution.py:13
  20.4 322.0 %reduce-scatter.2.cloned.1.call-start = ((), (), s32[]{:S(2)}) async-start(), calls=%async_computation.2 | async-start | bytes 3194880 | tf_op jit(solution)/shard_map/reduce_scatter | solution.py:25
  77.8 1.4 copy-start.1
Sparse Core Ops, SparseCore 0:
  20.5 51.6 all-gather.1
  78.0 225.9 reduce-scatter.1
where the time goes:
time: 351 us
  blocking collectives  268 us (76%)
  waiting for transfers between devices  51.2 us (15%)
  between operations  14.7 us (4%)
  matrix products  13.7 us (4%)
    psum x1, blocking collectives, on_device(): input_sum = lax.psum(partial_terms, REP)  255 us
    all_gather x1, waiting for transfers between devices, whole_of(): nearer = lax.all_gather(array, axes[-1], axis=dim, tiled=True)  51.1 us
    all_gather x1, blocking collectives, whole_of(): nearer = lax.all_gather(array, axes[-1], axis=dim, tiled=True)  13.1 us
    dot_general x1, matrix products, on_device(): jnp.dot(pre_grad, up_weight, preferred_element_type=jnp.float32)  8.12 us
  transfers between devices with their start and end apart: 2, of which 1 were waited for; matrix products, arithmetic and copies ran while one was open for 2% of the time, Pallas kernels for 0%

commit v1 on v0

--- a/solution.py
+++ b/solution.py
@@ -34,7 +34,8 @@
     hidden_grad = jnp.dot(grad_live, down_weight, preferred_element_type=jnp.float32)
     pre_grad = jnp.where(pre_act > 0, hidden_grad, jnp.zeros_like(hidden_grad)).astype(jnp.bfloat16)
     partial_terms = jnp.dot(pre_grad, up_weight, preferred_element_type=jnp.float32)
-    input_sum = lax.psum(partial_terms, REP)
+    one_axis = lax.psum(partial_terms, "rep_0")
+    input_sum = lax.psum(one_axis, "rep_1")
     input_grad = input_sum.astype(jnp.bfloat16)
     return (input_grad, down_grad)
 

time: 351 us -> 593 us (1.69)
  waiting for transfers between devices: 51.2 us -> 401 us
  blocking collectives: 268 us -> 161 us
    reduce_scatter x1, waiting for transfers between devices: 0.01 us -> 208 us  [on_device(): lax.psum_scatter(lax.dot_general(grad_live, hidden, (((0,), (0,)), ((), (...]
    psum x0 -> x1, waiting for transfers between devices: none -> 141 us  [on_device(): one_axis = lax.psum(partial_terms, 'rep_0')]
    psum x1, blocking collectives: 255 us -> 148 us  [on_device(): input_sum = lax.psum(one_axis, 'rep_1')]
  transfers between devices with their start and end apart: 2 -> 3, of which waited for: 1 -> 3; matrix products, arithmetic and copies ran while one was open for 2% -> 2% of each run, Pallas kernels for 0% -> 0%
where the time goes in v1:
time: 593 us; the launch traced here: 592 us
  waiting for transfers between devices  401 us (68%)
  blocking collectives  161 us (27%)
  between operations  14.4 us (2%)
  matrix products  13.8 us (2%)
    reduce_scatter x1, waiting for transfers between devices, on_device(): lax.psum_scatter(lax.dot_general(grad_live, hidden, (((0,), (0,)), ((), (...  208 us
    psum x1, blocking collectives, on_device(): input_sum = lax.psum(one_axis, 'rep_1')  148 us
    psum x1, waiting for transfers between devices, on_device(): one_axis = lax.psum(partial_terms, 'rep_0')  141 us
    all_gather x1, waiting for transfers between devices, whole_of(): nearer = lax.all_gather(array, axes[-1], axis=dim, tiled=True)  51.1 us
    all_gather x1, blocking collectives, whole_of(): nearer = lax.all_gather(array, axes[-1], axis=dim, tiled=True)  13.1 us
  transfers between devices with their start and end apart: 3, of which 3 were waited for; matrix products, arithmetic and copies ran while one was open for 2% of the time, Pallas kernels for 0%

profile of v1, /device:TPU:4, one launch (start us, length us, event | category | flops | bytes accessed | tf_op | source)
XLA Modules:
  0.0 592.3 jit_solution(3514502417053361099)
XLA Ops:
  7.2 0.0 copy-start
  7.2 0.0 all-gather.2.cloned.1.call-start
  7.2 13.1 %all_gather.6 = bf16[768,512]{1,0:T(8,128)(2,1)} all-gather(bf16[768,256]{1,0:T(8,128)(2,1)} %param.5), channel_id=1, replica_groups=mesh['dp'=64,'rep_0'=4,'rep_1'=2] {'rep_1'}, dimensions={1}, use_global_device_ids=true | all-gather | bytes 1179648 | tf_op jit(solution)/shard_map/all_gather | solution.py:13
  20.3 0.0 all-gather.2.cloned.1.call-update
  20.4 0.0 reduce-scatter.2.cloned.1.call-start
  21.1 51.1 %all-gather.2.cloned.1.call-done = bf16[768,2048]{1,0:T(8,128)(2,1)} async-done(((bf16[768,512]{1,0:T(8,128)(2,1)}), bf16[768,2048]{1,0:T(8,128)(2,1)}) %all-gather.2.cloned.1.call-update) | async-done | bytes 3145744 | tf_op jit(solution)/shard_map/all_gather | solution.py:13
  72.2 5.7 fusion.1
  77.9 0.0 copy-start.1
  77.9 0.0 reduce-scatter.2.cloned.1.call-update
  77.9 0.0 all-reduce.3.cloned.1.call-start
  77.9 0.0 copy-done
  77.9 1.3 copy-done.1
  79.3 8.1 %fusion.2 = f32[768,2048]{1,0:T(8,128)} fusion(bf16[384,2048]{1,0:T(8,128)(2,1)S(1)} %copy-done, bf16[2048,384]{1,0:T(8,128)(2,1)S(1)} %copy-done.1, bf16[768,2048]{1,0:T(8,128)(2,1)} %all-gather.2.cloned.1.call-done, pred[768]{0:T(1024)(128)(4,1)S(1)} %iota_compare_fusion, bf16[768,384]{1,0:T(8,128)(2,1)} %param.6), kind=kOutput, calls=%fused_computation.4 | convolution fusion | flops 2418376704 | bytes 13173504 | tf_op jit(solution)/shard_map/dot_general | solution.py:36
  87.4 0.0 all-reduce.3.cloned.1.call-update
  87.4 208.0 %reduce-scatter.2.cloned.1.call-done = f32[32,384]{1,0:T(8,128)} async-done(((f32[2048,384]{1,0:T(8,128)}), f32[32,384]{1,0:T(8,128)}) %reduce-scatter.2.cloned.1.call-update) | async-done | bytes 49168 | tf_op jit(solution)/shard_map/reduce_scatter | solution.py:25
  295.4 1.4 broadcast_multiply_fusion
  296.8 141.5 %all-reduce.3.cloned.1.call-done = f32[768,2048]{1,0:T(8,128)} async-done(((f32[768,2048]{1,0:T(8,128)}), f32[768,2048]{1,0:T(8,128)}) %all-reduce.3.cloned.1.call-update) | async-done | bytes 6291472 | tf_op jit(solution)/shard_map/psum | solution.py:37
  438.3 147.5 %all-reduce.4 = bf16[768,2048]{1,0:T(8,128)(2,1)} all-reduce(f32[768,2048]{1,0:T(8,128)} %all-reduce.3.cloned.1.call-done), channel_id=1, replica_groups=mesh['dp'=64,'rep_0'=4,'rep_1'=2] {'rep_1'}, use_global_device_ids=true, to_apply=%region_1.2 | all-reduce | flops 1572864 | bytes 9437184 | tf_op jit(solution)/shard_map/psum | solution.py:38
  (1 shorter events, 0.0 us)
Async XLA Ops:
  7.2 70.8 %copy-start = (bf16[384,2048]{1,0:T(8,128)(2,1)S(1)}, bf16[384,2048]{1,0:T(8,128)(2,1)}, u32[]{:S(2)}) copy-start(bf16[384,2048]{1,0:T(8,128)(2,1)} %param.7) | copy-start | bytes 4718596
  7.2 65.0 %all-gather.2.cloned.1.call-start = ((), (), s32[]{:S(2)}) async-start(), calls=%async_computation.1 | async-start | bytes 3932160 | tf_op jit(solution)/shard_map/all_gather | solution.py:13
  20.4 275.0 %reduce-scatter.2.cloned.1.call-start = ((), (), s32[]{:S(2)}) async-start(), calls=%async_computation.3 | async-start | bytes 3194880 | tf_op jit(solution)/shard_map/reduce_scatter | solution.py:25
  77.9 1.4 copy-start.1
  77.9 360.4 %all-reduce.3.cloned.1.call-start = ((), (), s32[]{:S(2)}) async-start(), calls=%async_computation.2 | async-start | bytes 12582912 | tf_op jit(solution)/shard_map/psum | solution.py:37
Sparse Core Ops, SparseCore 0:
  20.5 51.6 all-gather.1
  78.0 217.3 reduce-scatter.1
  297.8 140.4 all-reduce.2
